TPU v7x, 32 devices: a whole 2x2x4 slice. The times are simulated.
32 devices in a mesh: dp: 16 (over z, y, core), tensor: 2 (over x).
Axes of the slice: x: 2, y: 2, z: 4, core: 2. Of those that a mesh axis runs over, the one named last changes fastest.
Arguments:
- inputs: bfloat16 [1024, 16, 1024], P('tensor', 'dp'), may hold values from -6 to 6
- segment_ids: int32 [1024, 16], P(None, 'dp'), may hold values from 0 to 512, as said below
- first_gain: bfloat16 [1024], replicated, may hold values from 0.25 to 1.75
- first_shift: bfloat16 [1024], replicated, may hold values from -1.75 to 1.75
- qkv_weight: bfloat16 [1024, 3, 1024], P(None, None, 'tensor'), may hold values from -0.1875 to 0.1875
- qv_bias: bfloat16 [2, 1024], P(None, 'tensor'), may hold values from -3 to 3
- out_weight: bfloat16 [1024, 1024], P('tensor'), may hold values from -1 to 1
- out_bias: bfloat16 [1024], replicated, may hold values from -3 to 3
- second_gain: bfloat16 [1024], replicated, may hold values from 0.25 to 1.75
- second_shift: bfloat16 [1024], replicated, may hold values from -1.75 to 1.75
- up_weight: bfloat16 [1024, 4096], P(None, 'tensor'), may hold values from -0.1875 to 0.1875
- up_bias: bfloat16 [4096], P('tensor'), may hold values from -3 to 3
- down_weight: bfloat16 [4096, 1024], P('tensor'), may hold values from -0.09375 to 0.09375
- down_bias: bfloat16 [1024], replicated, may hold values from -3 to 3
- cotangent: bfloat16 [1024, 16, 1024], P('tensor', 'dp'), may hold values from -6 to 6
Outputs:
- layer_output: bfloat16 [1024, 16, 1024], P('tensor', 'dp')
- input_grad: float32 [1024, 16, 1024], P('tensor', 'dp')
- first_gain_grad: float32 [1024], replicated
- first_shift_grad: float32 [1024], replicated
- qkv_weight_grad: float32 [1024, 3, 1024], P('dp', None, 'tensor')
- qv_bias_grad: float32 [2, 1024], P(None, 'tensor')
- out_weight_grad: float32 [1024, 1024], P('tensor', 'dp')
- out_bias_grad: float32 [1024], replicated
- second_gain_grad: float32 [1024], replicated
- second_shift_grad: float32 [1024], replicated
- up_weight_grad: float32 [1024, 4096], P('dp', 'tensor')
- up_bias_grad: float32 [4096], P('tensor')
- down_weight_grad: float32 [4096, 1024], P('tensor', 'dp')
- down_bias_grad: float32 [1024], replicated
Inputs may be any that keep to these rules, and one draw needn't show every extreme that they name: `segment_ids`: along each sequence the ids start at 0, never fall and rise by one at the start of each new document. Each sequence has one long document that starts at one of its first 257 positions and ends at one of its last 257 positions; the others are short. In one sequence, chosen by the seed, every position outside the long document is a document of its own.
All inputs are finite; a program needn't handle non-finite values.
Results may differ from a plain program's by a relative error of at most 0.012.
The roundings to bfloat16 on the way count: a program that leaves them out, or rounds other values in their place, can miss the bound.
Values may be sent and summed in bfloat16 or wider, within the bound.
A program may use at most 192 MiB of HBM per device.

v0:
```python
import jax
import jax.numpy as jnp
from jax import lax
from jax.sharding import PartitionSpec as P

HEAD_DIM = 64


norm_eps = 1e-05


def layer_norm(value, gain, shift):
    row_mean = jnp.mean(value, axis=-1, keepdims=True)
    centred = value - row_mean
    variance = jnp.mean(centred * centred, axis=-1, keepdims=True)
    return centred * lax.rsqrt(variance + norm_eps) * gain + shift


def gelu_tanh(value):
    return (
        0.5
        * value
        * (1.0 + jnp.tanh(0.7978845608028654 * (value + 0.044715 * value * value * value)))
    )


def masked_scores(query_block, keys_all, seg_block, seg_all, row_start, block_rows, score_scale):
    scores = (
        jnp.einsum("qhd,khd->hqk", query_block, keys_all, preferred_element_type=jnp.float32)
        * score_scale
    )
    key_pos = jnp.arange(keys_all.shape[0], dtype=jnp.int32)
    query_pos = row_start + jnp.arange(block_rows, dtype=jnp.int32)
    allowed = (seg_block[:, None] == seg_all[None, :]) & (query_pos[:, None] >= key_pos[None, :])
    return jnp.where(allowed[None], scores, -1e30)


def attend_forward(queries, keys_all, values_all, seg_all, score_scale):
    seq_len = queries.shape[0]
    block_rows = min(512, seq_len)

    def one_block(block_index):
        row_start = block_index * block_rows
        query_block = lax.dynamic_slice_in_dim(queries, row_start, block_rows, 0)
        seg_block = lax.dynamic_slice_in_dim(seg_all, row_start, block_rows, 0)
        scores = masked_scores(
            query_block, keys_all, seg_block, seg_all, row_start, block_rows, score_scale
        )
        row_top = jnp.max(scores, axis=-1, keepdims=True)
        weights = jnp.exp(scores - row_top)
        row_total = jnp.sum(weights, axis=-1, keepdims=True)
        probs_low = (weights / row_total).astype(jnp.bfloat16)
        mixed = jnp.einsum(
            "hqk,khd->qhd", probs_low, values_all, preferred_element_type=jnp.float32
        )
        return (mixed, row_top + jnp.log(row_total))

    mixed, log_total = lax.map(one_block, jnp.arange(seq_len // block_rows, dtype=jnp.int32))
    return (mixed.reshape(seq_len, -1), log_total)


def attend_backward(queries, keys_all, values_all, seg_all, log_total, out_grad, score_scale):
    seq_len = queries.shape[0]
    block_rows = min(512, seq_len)

    def one_block(carry, block_index):
        key_grad, value_grad = carry
        row_start = block_index * block_rows
        query_block = lax.dynamic_slice_in_dim(queries, row_start, block_rows, 0)
        seg_block = lax.dynamic_slice_in_dim(seg_all, row_start, block_rows, 0)
        grad_block = lax.dynamic_slice_in_dim(out_grad, row_start, block_rows, 0)
        scores = masked_scores(
            query_block, keys_all, seg_block, seg_all, row_start, block_rows, score_scale
        )
        probs = jnp.exp(scores - log_total[block_index])
        probs_low = probs.astype(jnp.bfloat16)
        value_grad = value_grad + jnp.einsum(
            "hqk,qhd->khd", probs_low, grad_block, preferred_element_type=jnp.float32
        )
        prob_grad = jnp.einsum(
            "qhd,khd->hqk", grad_block, values_all, preferred_element_type=jnp.float32
        )
        row_dot = jnp.sum(probs * prob_grad, axis=-1, keepdims=True)
        score_grad = (probs * (prob_grad - row_dot)).astype(jnp.bfloat16)
        query_grad = (
            jnp.einsum("hqk,khd->qhd", score_grad, keys_all, preferred_element_type=jnp.float32)
            * score_scale
        )
        key_grad = (
            key_grad
            + jnp.einsum(
                "hqk,qhd->khd", score_grad, query_block, preferred_element_type=jnp.float32
            )
            * score_scale
        )
        return ((key_grad, value_grad), query_grad)

    zero_grads = jnp.zeros(keys_all.shape, jnp.float32)
    (key_grad, value_grad), query_grad = lax.scan(
        one_block, (zero_grads, zero_grads), jnp.arange(seq_len // block_rows, dtype=jnp.int32)
    )
    return (
        query_grad.reshape(seq_len, -1),
        key_grad.reshape(seq_len, -1),
        value_grad.reshape(seq_len, -1),
    )


def row_product(left, right, contract):
    return lax.dot_general(
        left, right, (((1,), (contract,)), ((), ())), preferred_element_type=jnp.float32
    )


def rows_contract(left, right):
    return lax.dot_general(
        left, right, (((0,), (0,)), ((), ())), preferred_element_type=jnp.float32
    )


def on_device(
    inputs,
    segment_ids,
    first_gain,
    first_shift,
    qkv_weight,
    qv_bias,
    out_weight,
    out_bias,
    second_gain,
    second_shift,
    up_weight,
    up_bias,
    down_weight,
    down_bias,
    cotangent,
):
    rows_dev, seq_count, model_width = inputs.shape
    tensor_count = lax.axis_size("tensor")
    tensor_rank = lax.axis_index("tensor")
    seq_len = rows_dev * tensor_count
    local_width = out_weight.shape[0]
    heads_dev = local_width // HEAD_DIM
    hidden_dev = up_weight.shape[1]
    local_rows = rows_dev * seq_count
    score_scale = HEAD_DIM ** (-0.5)
    residual_in = inputs.reshape(local_rows, model_width).astype(jnp.float32)
    gain_one = first_gain.astype(jnp.float32)
    shift_one = first_shift.astype(jnp.float32)
    gain_two = second_gain.astype(jnp.float32)
    shift_two = second_shift.astype(jnp.float32)
    normed_one, pull_one = jax.vjp(layer_norm, residual_in, gain_one, shift_one)
    first_local = normed_one.astype(jnp.bfloat16)
    first_rows = lax.all_gather(first_local, "tensor", axis=0, tiled=True)
    qkv_flat = qkv_weight.reshape(model_width, 3 * local_width)
    qkv_bias = jnp.concatenate(
        [
            qv_bias[0].astype(jnp.float32),
            jnp.zeros((local_width,), jnp.float32),
            qv_bias[1].astype(jnp.float32),
        ]
    )
    qkv_low = (jnp.dot(first_rows, qkv_flat, preferred_element_type=jnp.float32) + qkv_bias).astype(
        jnp.bfloat16
    )
    qkv_split = qkv_low.reshape(seq_len, seq_count, 3, heads_dev, HEAD_DIM)
    seq_index = 0
    mixed_one, log_one = attend_forward(
        qkv_split[:, seq_index, 0],
        qkv_split[:, seq_index, 1],
        qkv_split[:, seq_index, 2],
        segment_ids[:, seq_index],
        score_scale,
    )
    mixed_list = [mixed_one]
    log_list = [log_one]
    mixed_low = (
        jnp.stack(mixed_list, axis=1).reshape(seq_len * seq_count, local_width).astype(jnp.bfloat16)
    )
    attn_local = lax.psum_scatter(
        row_product(mixed_low, out_weight, 0), "tensor", scatter_dimension=0, tiled=True
    )
    residual_mid = residual_in + attn_local + out_bias.astype(jnp.float32)
    normed_two, pull_two = jax.vjp(layer_norm, residual_mid, gain_two, shift_two)
    second_local = normed_two.astype(jnp.bfloat16)
    second_rows = lax.all_gather(second_local, "tensor", axis=0, tiled=True)
    hidden_pre = jnp.dot(
        second_rows, up_weight, preferred_element_type=jnp.float32
    ) + up_bias.astype(jnp.float32)
    activated, pull_gelu = jax.vjp(gelu_tanh, hidden_pre)
    hidden_low = activated.astype(jnp.bfloat16)
    mlp_local = lax.psum_scatter(
        row_product(hidden_low, down_weight, 0).astype(jnp.bfloat16),
        "tensor",
        scatter_dimension=0,
        tiled=True,
    ).astype(jnp.float32)
    layer_output = (residual_mid + mlp_local + down_bias.astype(jnp.float32)).astype(jnp.bfloat16)
    layer_output = layer_output.reshape(rows_dev, seq_count, model_width)
    grad_local = cotangent.reshape(local_rows, model_width)
    grad_rows = lax.all_gather(grad_local, "tensor", axis=0, tiled=True)
    down_grad = rows_contract(hidden_low, grad_rows)
    hidden_grad = lax.dot_general(
        grad_rows, down_weight, (((1,), (1,)), ((), ())), preferred_element_type=jnp.float32
    )
    (pre_grad,) = pull_gelu(hidden_grad)
    pre_low = pre_grad.astype(jnp.bfloat16)
    up_sums = jnp.sum(pre_low, axis=0, dtype=jnp.float32)
    second_back = lax.all_gather(second_local, "tensor", axis=0, tiled=True)
    up_grad = rows_contract(second_back, pre_low)
    second_norm_grad = lax.psum_scatter(
        row_product(pre_low, up_weight, 1), "tensor", scatter_dimension=0, tiled=True
    )
    mid_from_norm, gain_two_grad, shift_two_grad = pull_two(second_norm_grad)
    residual_grad = grad_local.astype(jnp.float32) + mid_from_norm
    residual_low = residual_grad.astype(jnp.bfloat16)
    residual_rows = lax.all_gather(residual_low, "tensor", axis=0, tiled=True)
    out_grad_weight = rows_contract(mixed_low, residual_rows)
    mixed_grad = lax.dot_general(
        residual_rows, out_weight, (((1,), (1,)), ((), ())), preferred_element_type=jnp.float32
    ).astype(jnp.bfloat16)
    mixed_grad = mixed_grad.reshape(seq_len, seq_count, heads_dev, HEAD_DIM)
    seq_index = 0
    query_grad, key_grad, value_grad = attend_backward(
        qkv_split[:, seq_index, 0],
        qkv_split[:, seq_index, 1],
        qkv_split[:, seq_index, 2],
        segment_ids[:, seq_index],
        log_list[seq_index],
        mixed_grad[:, seq_index],
        score_scale,
    )
    query_list = [query_grad]
    key_list = [key_grad]
    value_list = [value_grad]
    qkv_grad = jnp.concatenate(
        [jnp.stack(query_list, axis=1), jnp.stack(key_list, axis=1), jnp.stack(value_list, axis=1)],
        axis=-1,
    )
    qkv_grad_low = qkv_grad.reshape(seq_len * seq_count, 3 * local_width).astype(jnp.bfloat16)
    qkv_sums = jnp.sum(qkv_grad_low, axis=0, dtype=jnp.float32)
    qv_sums = jnp.stack([qkv_sums[:local_width], qkv_sums[2 * local_width :]], axis=0)
    first_back = lax.all_gather(first_local, "tensor", axis=0, tiled=True)
    qkv_grad_weight = rows_contract(first_back, qkv_grad_low).reshape(model_width, 3, local_width)
    first_norm_grad = lax.psum_scatter(
        row_product(qkv_grad_low, qkv_flat, 1), "tensor", scatter_dimension=0, tiled=True
    )
    in_from_norm, gain_one_grad, shift_one_grad = pull_one(first_norm_grad)
    input_grad = (residual_grad + in_from_norm).reshape(rows_dev, seq_count, model_width)
    qkv_share, out_share, up_share, down_share = (
        lax.psum_scatter(qkv_grad_weight, "dp", scatter_dimension=0, tiled=True),
        lax.psum_scatter(out_grad_weight, "dp", scatter_dimension=1, tiled=True),
        lax.psum_scatter(up_grad, "dp", scatter_dimension=0, tiled=True),
        lax.psum_scatter(down_grad, "dp", scatter_dimension=1, tiled=True),
    )
    out_bias_part = jnp.sum(residual_low, axis=0, dtype=jnp.float32)
    down_bias_part = jnp.sum(grad_local, axis=0, dtype=jnp.float32)
    stacked = jnp.stack(
        [
            gain_one_grad,
            shift_one_grad,
            gain_two_grad,
            shift_two_grad,
            out_bias_part,
            down_bias_part,
        ],
        axis=0,
    )
    qv_full = lax.dynamic_update_slice(
        jnp.zeros((2, model_width), jnp.float32), qv_sums, (jnp.int32(0), tensor_rank * local_width)
    )
    up_full = lax.dynamic_update_slice(
        jnp.zeros((hidden_dev * tensor_count,), jnp.float32), up_sums, (tensor_rank * hidden_dev,)
    )
    stacked, qv_total, up_total = lax.psum((stacked, qv_full, up_full), ("dp", "tensor"))
    qv_share = lax.dynamic_slice_in_dim(qv_total, tensor_rank * local_width, local_width, 1)
    up_bias_share = lax.dynamic_slice_in_dim(up_total, tensor_rank * hidden_dev, hidden_dev, 0)
    return (
        layer_output,
        input_grad,
        stacked[0],
        stacked[1],
        qkv_share,
        qv_share,
        out_share,
        stacked[4],
        stacked[2],
        stacked[3],
        up_share,
        up_bias_share,
        down_share,
        stacked[5],
    )


def solution(mesh):
    in_specs = (
        P("tensor", "dp", None),
        P(None, "dp"),
        P(),
        P(),
        P(None, None, "tensor"),
        P(None, "tensor"),
        P("tensor", None),
        P(),
        P(),
        P(),
        P(None, "tensor"),
        P("tensor"),
        P("tensor", None),
        P(),
        P("tensor", "dp", None),
    )
    out_specs = (
        P("tensor", "dp", None),
        P("tensor", "dp", None),
        P(),
        P(),
        P("dp", None, "tensor"),
        P(None, "tensor"),
        P("tensor", "dp"),
        P(),
        P(),
        P(),
        P("dp", "tensor"),
        P("tensor"),
        P("tensor", "dp"),
        P(),
    )
    return jax.shard_map(
        on_device, mesh=mesh, in_specs=in_specs, out_specs=out_specs, check_vma=False
    )
```

profile of v0, /device:TPU:0, one launch (start us, length us, event | category | flops | bytes accessed | tf_op | source)
XLA Modules:
  0.0 929.0 jit_solution(7971377739620358646)
XLA Ops:
  19.8 31.2 %all-gather.6.cloned.1.call-done = bf16[1024,1024]{1,0:T(8,128)(2,1)} async-done(((bf16[512,1024]{1,0:T(8,128)(2,1)}), bf16[1024,1024]{1,0:T(8,128)(2,1)}) %all-gather.6.cloned.1.call-update) | async-done | bytes 2097168 | tf_op jit(solution)/shard_map/all_gather | solution.py:154
  67.7 32.5 %while.27 = (s32[]{:T(128)}, bf16[2,512,8,64]{1,3,2,0:T(8,128)(2,1)}, f32[2,8,512,1]{2,1,3,0:T(8,128)S(1)}, s32[2]{0:T(128)S(1)}, s32[1024]{0:T(1024)S(1)}, /*in...) while((s32[]{:T(128)}, ...), condition=%wide.region_5.6_spmd, body=%wide.region_2.5_spmd.sunk | while | flops 1125642752 | bytes 64633100 | solution.py:58
  107.8 53.8 %reduce-scatter.9.cloned.1.call-done = f32[512,1024]{1,0:T(8,128)} async-done(((f32[1024,1024]{1,0:T(8,128)}), f32[512,1024]{1,0:T(8,128)}) %reduce-scatter.9.cloned.1.call-update) | async-done | bytes 2097168 | tf_op jit(solution)/shard_map/reduce_scatter | solution.py:180
  167.2 32.6 %all-gather.8.cloned.1.call-done = bf16[1024,1024]{1,0:T(8,128)(2,1)} async-done(((bf16[512,1024]{1,0:T(8,128)(2,1)}), bf16[1024,1024]{1,0:T(8,128)(2,1)}) %all-gather.8.cloned.1.call-update) | async-done | bytes 2097168 | tf_op jit(solution)/shard_map/all_gather | solution.py:186
  199.8 10.9 %fusion.76 = f32[1024,2048]{1,0:T(8,128)} fusion(bf16[1024,1024]{1,0:T(8,128)(2,1)} %all-gather.8.cloned.1.call-done, bf16[1024,2048]{1,0:T(8,128)(2,1)} %param.29), kind=kOutput, calls=%fused_computation.125 | convolution fusion | flops 4294967296 | bytes 14680064 | tf_op jit(solution)/shard_map/dot_general | solution.py:187
  210.7 23.7 %all-gather.12.cloned.1.call-done = bf16[1024,1,1024]{2,0,1:T(8,128)(2,1)} async-done(((bf16[512,1,1024]{2,0,1:T(8,128)(2,1)}), bf16[1024,1,1024]{2,0,1:T(8,128)(2,1)}) %all-gather.12.cloned.1.call-update) | async-done | bytes 2097168 | tf_op jit(solution)/shard_map/all_gather | solution.py:201
  234.4 15.1 %convert_reduce_fusion = (f32[2048]{0:T(1024)}, bf16[1024,2048]{1,0:T(8,128)(2,1)S(1)}) fusion(bf16[2048,1024]{1,0:T(8,128)(2,1)} %param.31, bf16[1024,1,1024]{2,0,1:T(8,128)(2,1)} %all-gather.12.cloned.1.call-done, f32[1024,2048]{1,0:T(8,128)} %fusion.76, f32[2048]{0:T(1024)S(1)} %convert_element_type.121), kind=kOutput, calls=%fused_computation.50 | convolution fusion | flops 4351588352 | bytes 18890752 | tf_op jit(solution)/shard_map/dot_general | solution.py:203
  257.7 11.2 %convolution_convert_fusion = bf16[1024,1024]{1,0:T(8,128)(2,1)} fusion(bf16[2048,1024]{1,0:T(8,128)(2,1)} %param.31, f32[1024,2048]{1,0:T(8,128)} %fusion.76, f32[2048]{0:T(1024)S(1)} %convert_element_type.121), kind=kOutput, calls=%fused_computation.95 | convolution fusion | flops 4316987392 | bytes 14688256 | tf_op jit(solution)/shard_map/dot_general | solution.py:110
  269.1 43.1 %reduce-scatter.13.cloned.1.call-done = f32[512,1024]{1,0:T(8,128)} async-done(((f32[1024,1024]{1,0:T(8,128)}), f32[512,1024]{1,0:T(8,128)}) %reduce-scatter.13.cloned.1.call-update) | async-done | bytes 2097168 | tf_op jit(solution)/shard_map/reduce_scatter | solution.py:211
  315.7 30.4 %reduce-scatter.11.cloned.1.call-done = bf16[512,1024]{1,0:T(8,128)(2,1)} async-done(((bf16[1024,1024]{1,0:T(8,128)(2,1)}), bf16[512,1024]{1,0:T(8,128)(2,1)}) %reduce-scatter.11.cloned.1.call-update) | async-done | bytes 1048592 | tf_op jit(solution)/shard_map/reduce_scatter | solution.py:192
  353.9 33.2 %all-gather.10.cloned.1.call-done = bf16[1024,1024]{1,0:T(8,128)(2,1)} async-done(((bf16[512,1024]{1,0:T(8,128)(2,1)}), bf16[1024,1024]{1,0:T(8,128)(2,1)}) %all-gather.10.cloned.1.call-update) | async-done | bytes 2097168 | tf_op jit(solution)/shard_map/all_gather | solution.py:217
  392.1 89.9 %while.28 = (s32[]{:T(128)}, f32[1024,8,64]{0,2,1:T(8,128)}, f32[1024,8,64]{0,2,1:T(8,128)}, bf16[2,512,8,64]{1,3,2,0:T(8,128)(2,1)}, s32[2]{0:T(128)S(1)}, /*in...) while((s32[]{:T(128)}, f32[1024,8,64]{0,2,1:T(8,128)}, ...), condition=%wide.region_15.16_spmd.clone, body=%wide.region_13.15_spmd.clone.sunk | while | flops 2726556160 | bytes 204831312 | solution.py:99
  400.0 11.6 %multiply_reduce_fusion.5 = (f32[8,512]{1,0:T(8,128)}, f32[8,512,1024]{2,1,0:T(8,128)}) fusion(f32[8,512,1024]{2,1,0:T(8,128)S(1)} %fusion.138, f32[8,512]{1,0:T(8,128)S(1)} %dynamic-slice_bitcast_fusion.2, bf16[1024,8,64]{0,2,1:T(8,128)(2,1)} %copy-done.3, bf16[1024,8,64]{0,2,1:T(8,128)(2,1)} %copy-done.5, s32[]{:T(128)S(6)} %select_n.57, ...), kind=kOutput, calls=%fused_computation.18.clone.1 | convolution fusion | flops 557838336 | bytes 35684356 | tf_op jit(solution)/shard_map/while/body/eval_jaxpr/qhd,khd->hqk/dot_general | solution.py:29
  411.6 9.4 %multiply_convert_fusion.5 = bf16[8,512,1024]{2,1,0:T(8,128)(2,1)} fusion(f32[8,512,1024]{2,1,0:T(8,128)} %get-tuple-element.412, f32[8,512,1024]{2,1,0:T(8,128)S(1)} %fusion.138, f32[8,512]{1,0:T(8,128)} %get-tuple-element.413), kind=kLoop, calls=%fused_computation.17.clone.1 | loop fusion | flops 12582912 | bytes 41959424 | tf_op jit(solution)/shard_map/while/body/eval_jaxpr/convert_element_type | solution.py:84
  443.7 11.6 %multiply_reduce_fusion.5 = (f32[8,512]{1,0:T(8,128)}, f32[8,512,1024]{2,1,0:T(8,128)}) fusion(f32[8,512,1024]{2,1,0:T(8,128)S(1)} %fusion.138, f32[8,512]{1,0:T(8,128)S(1)} %dynamic-slice_bitcast_fusion.2, bf16[1024,8,64]{0,2,1:T(8,128)(2,1)} %copy-done.3, bf16[1024,8,64]{0,2,1:T(8,128)(2,1)} %copy-done.5, s32[]{:T(128)S(6)} %select_n.57, ...), kind=kOutput, calls=%fused_computation.18.clone.1 | convolution fusion | flops 557838336 | bytes 35684356 | tf_op jit(solution)/shard_map/while/body/eval_jaxpr/qhd,khd->hqk/dot_general | solution.py:29
  464.7 9.5 %bitcast_add_fusion.5 = f32[1024,8,64]{0,2,1:T(8,128)} fusion(f32[1024,8,64]{0,2,1:T(8,128)} %get-tuple-element.472, f32[8,512,1024]{2,1,0:T(8,128)} %get-tuple-element.412, pred[]{:T(512)S(6)} %compare.3, bf16[1024,8,64]{0,2,1:T(8,128)(2,1)S(1)} %copy-done.9, s32[]{:T(128)S(6)} %select_n.57), kind=kOutput, calls=%fused_computation.22.clone.1 | convolution fusion | flops 542113792 | bytes 21495812 | tf_op jit(solution)/shard_map/while/body/eval_jaxpr/hqk,qhd->khd/dot_general | solution.py:77
  494.9 12.0 %fusion.56 = f32[2048,1024]{0,1:T(8,128)} fusion(bf16[1024,1,1024]{2,0,1:T(8,128)(2,1)} %all-gather.12.cloned.1.call-done, f32[1024,2048]{1,0:T(8,128)} %fusion.76, f32[2048]{0:T(1024)S(1)} %copy-done.41), kind=kOutput, calls=%fused_computation.84 | convolution fusion | flops 4315938816 | bytes 18882560 | tf_op jit(solution)/shard_map/dot_general | solution.py:116
  507.0 10.7 %fusion.79 = f32[1024,2048]{1,0:T(8,128)} fusion(bf16[1024,1024]{1,0:T(8,128)(2,1)} %all-gather.8.cloned.1.call-done, bf16[1024,2048]{1,0:T(8,128)(2,1)} %copy-done.51), kind=kOutput, calls=%fused_computation.128 | convolution fusion | flops 4294967296 | bytes 14680064 | tf_op jit(solution)/shard_map/dot_general | solution.py:116
  534.3 14.4 %reduce-scatter.15.cloned.1.call-done = f32[512,1024]{1,0:T(8,128)} async-done(((f32[1024,1024]{1,0:T(8,128)}), f32[512,1024]{1,0:T(8,128)}) %reduce-scatter.15.cloned.1.call-update) | async-done | bytes 2097168 | tf_op jit(solution)/shard_map/reduce_scatter | solution.py:245
  556.5 40.2 %all-reduce = (f32[6,1024]{1,0:T(8,128)S(1)}, f32[2,1024]{1,0:T(2,128)S(1)}, f32[4096]{0:T(1024)S(1)}) all-reduce(f32[6,1024]{1,0:T(8,128)S(1)} %stack.24, f32[2,1024]{1,0:T(2,128)S(1)} %maximum_dynamic-update-slice_fusion, f32[4096]{0:T(1024)S(1)} %dynamic_update_slice.18), channel_id=1, replica_groups=mesh['dp'=16,'tensor'=2] {'dp','tensor'}, use_global_device_ids=true, to_apply=%region_25.26 | all-reduce | flops 12288 | bytes 98304 | tf_op jit(solution)/shard_map/psum | solution.py:275
  598.5 59.5 %reduce-scatter.23.cloned.1.call-done = f32[2048,64]{0,1:T(8,128)} async-done(((f32[2048,1024]{0,1:T(8,128)}), f32[2048,64]{0,1:T(8,128)}) %reduce-scatter.23.cloned.1.call-update) | async-done | bytes 524304 | tf_op jit(solution)/shard_map/reduce_scatter | solution.py:254
  658.0 108.9 %reduce-scatter.21.cloned.1.call-done = f32[64,2048]{1,0:T(8,128)} async-done(((f32[1024,2048]{1,0:T(8,128)}), f32[64,2048]{1,0:T(8,128)}) %reduce-scatter.21.cloned.1.call-update) | async-done | bytes 524304 | tf_op jit(solution)/shard_map/reduce_scatter | solution.py:253
  766.9 65.7 %reduce-scatter.19.cloned.1.call-done = f32[512,64]{0,1:T(8,128)} async-done(((f32[512,1024]{0,1:T(8,128)}), f32[512,64]{0,1:T(8,128)}) %reduce-scatter.19.cloned.1.call-update) | async-done | bytes 131088 | tf_op jit(solution)/shard_map/reduce_scatter | solution.py:252
  832.6 89.1 %reduce-scatter.17.cloned.1.call-done = f32[64,3,512]{2,0,1:T(8,128)} async-done(((f32[1024,3,512]{2,0,1:T(8,128)}), f32[64,3,512]{2,0,1:T(8,128)}) %reduce-scatter.17.cloned.1.call-update) | async-done | bytes 393232 | tf_op jit(solution)/shard_map/reduce_scatter | solution.py:251
  (252 shorter events, 178.9 us)
Async XLA Ops:
  7.2 96.7 %copy-start = (bf16[512,1024]{1,0:T(8,128)(2,1)S(1)}, bf16[512,1024]{1,0:T(8,128)(2,1)}, u32[]{:S(2)}) copy-start(bf16[512,1024]{1,0:T(8,128)(2,1)} %param.25) | copy-start | bytes 3145732
  7.2 43.8 %all-gather.6.cloned.1.call-start = ((), (), s32[]{:S(2)}) async-start(), calls=%async_computation.8 | async-start | bytes 3145728 | tf_op jit(solution)/shard_map/all_gather | solution.py:154
  15.1 146.5 %reduce-scatter.9.cloned.1.call-start = ((), (), s32[]{:S(2)}) async-start(), calls=%async_computation.9 | async-start | bytes 6291456 | tf_op jit(solution)/shard_map/reduce_scatter | solution.py:180
  107.1 92.7 %all-gather.8.cloned.1.call-start = ((), (), s32[]{:S(2)}) async-start(), calls=%async_computation.10 | async-start | bytes 3145728 | tf_op jit(solution)/shard_map/all_gather | solution.py:186
  166.5 67.9 %all-gather.12.cloned.1.call-start = ((), (), s32[]{:S(2)}) async-start(), calls=%async_computation.19 | async-start | bytes 3145728 | tf_op jit(solution)/shard_map/all_gather | solution.py:201
  167.1 145.1 %reduce-scatter.13.cloned.1.call-start = ((), (), s32[]{:S(2)}) async-start(), calls=%async_computation.12 | async-start | bytes 6291456 | tf_op jit(solution)/shard_map/reduce_scatter | solution.py:211
  167.1 90.6 %copy-start.40 = (f32[2048]{0:T(1024)}, f32[2048]{0:T(1024)S(1)}, u32[]{:S(2)}) copy-start(f32[2048]{0:T(1024)S(1)} %convert_element_type.121) | copy-start | bytes 24580
  234.4 17.1 %copy-start.49 = (bf16[1024,2048]{1,0:T(8,128)(2,1)S(1)}, bf16[1024,2048]{1,0:T(8,128)(2,1)}, u32[]{:S(2)}) copy-start(bf16[1024,2048]{1,0:T(8,128)(2,1)} %param.29) | copy-start | bytes 12582916
  257.7 11.4 %copy-start.48 = (bf16[1024]{0:T(1024)(128)(2,1)S(1)}, bf16[1024]{0:T(1024)(128)(2,1)}, u32[]{:S(2)}) copy-start(bf16[1024]{0:T(1024)(128)(2,1)} %param.32) | copy-start | bytes 6148
  257.7 88.4 %reduce-scatter.11.cloned.1.call-start = ((), (), s32[]{:S(2)}) async-start(), calls=%async_computation.11 | async-start | bytes 3145728 | tf_op jit(solution)/shard_map/reduce_scatter | solution.py:192
  269.0 118.1 %all-gather.10.cloned.1.call-start = ((), (), s32[]{:S(2)}) async-start(), calls=%async_computation.13 | async-start | bytes 3145728 | tf_op jit(solution)/shard_map/all_gather | solution.py:217
  350.5 40.5 %copy-start.33 = (f32[512]{0:T(512)}, f32[512]{0:T(512)S(1)}, u32[]{:S(2)}) copy-start(f32[512]{0:T(512)S(1)} %negate_multiply_fusion.1) | copy-start | bytes 6148
  353.9 194.8 %reduce-scatter.15.cloned.1.call-start = ((), (), s32[]{:S(2)}) async-start(), calls=%async_computation.14 | async-start | bytes 6291456 | tf_op jit(solution)/shard_map/reduce_scatter | solution.py:245
  494.2 163.8 %reduce-scatter.23.cloned.1.call-start = ((), (), s32[]{:S(2)}) async-start(), calls=%async_computation.18 | async-start | bytes 8912896 | tf_op jit(solution)/shard_map/reduce_scatter | solution.py:254
  506.9 260.0 %reduce-scatter.21.cloned.1.call-start = ((), (), s32[]{:S(2)}) async-start(), calls=%async_computation.17 | async-start | bytes 8912896 | tf_op jit(solution)/shard_map/reduce_scatter | solution.py:253
  517.7 314.9 %reduce-scatter.19.cloned.1.call-start = ((), (), s32[]{:S(2)}) async-start(), calls=%async_computation.16 | async-start | bytes 2228224 | tf_op jit(solution)/shard_map/reduce_scatter | solution.py:252
  523.1 398.6 %reduce-scatter.17.cloned.1.call-start = ((), (), s32[]{:S(2)}) async-start(), calls=%async_computation.15 | async-start | bytes 6684672 | tf_op jit(solution)/shard_map/reduce_scatter | solution.py:251
  532.5 16.2 %copy-start.8 = (bf16[512,1,1024]{2,0,1:T(8,128)(2,1)S(1)}, bf16[512,1,1024]{2,0,1:T(8,128)(2,1)}, u32[]{:S(2)}) copy-start(bf16[512,1,1024]{2,0,1:T(8,128)(2,1)} %param.19) | copy-start | bytes 3145732
  532.5 16.2 %copy-start.28 = (f32[1024]{0:T(1024)S(1)}, f32[1024]{0:T(1024)}, u32[]{:S(2)}) copy-start(f32[1024]{0:T(1024)} %copy-done.27) | copy-start | bytes 12292
  532.5 16.2 %copy-start.30 = (f32[512]{0:T(512)S(1)}, f32[512]{0:T(512)}, u32[]{:S(2)}) copy-start(f32[512]{0:T(512)} %copy-done.29) | copy-start | bytes 6148
  532.5 18.4 %copy-start.36 = (f32[512]{0:T(512)S(1)}, f32[512]{0:T(512)}, u32[]{:S(2)}) copy-start(f32[512]{0:T(512)} %copy-done.35) | copy-start | bytes 6148
  532.6 18.4 %copy-start.32 = (f32[512]{0:T(512)S(1)}, f32[512]{0:T(512)}, u32[]{:S(2)}) copy-start(f32[512]{0:T(512)} %copy-done.31) | copy-start | bytes 6148
  534.3 17.7 %copy-start.34 = (f32[512]{0:T(512)S(1)}, f32[512]{0:T(512)}, u32[]{:S(2)}) copy-start(f32[512]{0:T(512)} %copy-done.33) | copy-start | bytes 6148
  552.0 369.7 %copy-start.1 = (bf16[512,1024]{1,0:T(8,128)(2,1)S(1)}, bf16[512,1024]{1,0:T(8,128)(2,1)}, u32[]{:S(2)}) copy-start(bf16[512,1024]{1,0:T(8,128)(2,1)} %param.25) | copy-start | bytes 3145732
  (52 other events, 186.9 us)
Sparse Core Ops, SparseCore 0:
  15.2 35.8 all-gather.5
  107.2 54.2 reduce-scatter.8
  166.6 33.1 all-gather.7
  201.2 33.1 all-gather.11
  257.8 54.3 reduce-scatter.12
  314.2 31.8 reduce-scatter.10
  354.0 33.1 all-gather.9
  494.3 54.3 reduce-scatter.14
  553.3 104.6 reduce-scatter.22
  662.5 104.3 reduce-scatter.20
  771.2 61.3 reduce-scatter.18
  837.5 84.2 reduce-scatter.16
where the time goes:
time: 939 us; the launch traced here: 929 us
  waiting for transfers between devices  586 us (62%)
  matrix products  176 us (19%)
  other arithmetic  60.7 us (6%)
  local copies, waits for them, and re-layouts  43.1 us (5%)
  blocking collectives  40.2 us (4%)
  between operations  15.1 us (2%)
    reduce_scatter x1, waiting for transfers between devices, on_device(): lax.psum_scatter(up_grad, 'dp', scatter_dimension=0, tiled=True)  109 us
    reduce_scatter x1, waiting for transfers between devices, on_device(): lax.psum_scatter(qkv_grad_weight, 'dp', scatter_dimension=0, tiled=True)  89.1 us
    reduce_scatter x1, waiting for transfers between devices, on_device(): lax.psum_scatter(out_grad_weight, 'dp', scatter_dimension=1, tiled=True)  65.7 us
    reduce_scatter x1, waiting for transfers between devices, on_device(): lax.psum_scatter(down_grad, 'dp', scatter_dimension=1, tiled=True)  59.5 us
    reduce_scatter x1, waiting for transfers between devices, on_device(): lax.psum_scatter(row_product(mixed_low, out_weight, 0), 'tensor', scatter...  53.8 us
    reduce_scatter x1, waiting for transfers between devices, on_device(): lax.psum_scatter(row_product(pre_low, up_weight, 1), 'tensor', scatter_di...  43.1 us
    psum x1, blocking collectives, on_device(): lax.psum((stacked, qv_full, up_full), ('dp', 'tensor'))  40.2 us
    all_gather x1, waiting for transfers between devices, on_device(): residual_rows = lax.all_gather(residual_low, 'tensor', axis=0, tiled=True)  33.2 us
  transfers between devices with their start and end apart: 12, of which 12 were waited for; matrix products, arithmetic and copies ran while one was open for 8% of the time, Pallas kernels for 0%

commit v1 on v0

--- a/solution.py
+++ b/solution.py
@@ -1,9 +1,17 @@
+import functools
+
 import jax
 import jax.numpy as jnp
 from jax import lax
+from jax.experimental import pallas as pl
+from jax.experimental.pallas import tpu as pltpu
 from jax.sharding import PartitionSpec as P
 
 HEAD_DIM = 64
+MESH = pl.DeviceIdType.MESH
+F32 = jnp.float32
+BF16 = jnp.bfloat16
+VMEM_LIMIT = 60 << 20
 
 
 norm_eps = 1e-05
@@ -293,6 +301,881 @@
     )
 
 
+Z_SIZE, Y_SIZE, CORES = 4, 2, 2
+
+
+def place():
+    dp = lax.axis_index("dp")
+    side = lax.axis_index("tensor")
+    return dp // 4, (dp // 2) % 2, dp % 2, side
+
+
+def dev(z, y, core, side):
+    return (z * 4 + y * 2 + core, side)
+
+
+def peer_x():
+    z, y, core, side = place()
+    return dev(z, y, core, 1 - side)
+
+
+def peer_y():
+    z, y, core, side = place()
+    return dev(z, 1 - y, core, side)
+
+
+def peer_core():
+    z, y, core, side = place()
+    return dev(z, y, 1 - core, side)
+
+
+def peer_z(step):
+    z, y, core, side = place()
+    return dev((z + step) % 4, y, core, side)
+
+
+def greet(peers):
+    barrier = pltpu.get_barrier_semaphore()
+    for peer in peers:
+        pl.semaphore_signal(barrier, inc=1, device_id=peer, device_id_type=MESH)
+    pl.semaphore_wait(barrier, len(peers))
+
+
+def remote(src, dst, send_sem, recv_sem, peer):
+    return pltpu.make_async_remote_copy(
+        src_ref=src, dst_ref=dst, send_sem=send_sem, recv_sem=recv_sem, device_id=peer, device_id_type=MESH
+    )
+
+
+def dot_nn(a, b):
+    return lax.dot_general(a, b, (((1,), (0,)), ((), ())), preferred_element_type=F32)
+
+
+def dot_nt(a, b):
+    return lax.dot_general(a, b, (((1,), (1,)), ((), ())), preferred_element_type=F32)
+
+
+def dot_tn(a, b):
+    return lax.dot_general(a, b, (((0,), (0,)), ((), ())), preferred_element_type=F32)
+
+
+def norm_parts(value):
+    mean = jnp.mean(value, axis=-1, keepdims=True)
+    centred = value - mean
+    rstd = lax.rsqrt(jnp.mean(centred * centred, axis=-1, keepdims=True) + norm_eps)
+    return centred * rstd, rstd
+
+
+def head_lanes(h):
+    lane = lax.broadcasted_iota(jnp.int32, (1, 2 * HEAD_DIM), 1)
+    return (lane // HEAD_DIM) == h
+
+
+def only_head(value, h):
+    return jnp.where(head_lanes(h), value, jnp.zeros_like(value))
+
+
+def attend_kernel(
+    x_ref, gain_ref, shift_ref, wqkv_ref, bias_ref, segc_ref, segr_ref, wout_ref, ob_ref,
+    a1_ref, qkv_ref, mix_ref, h_ref,
+    mask_ref, send_ref, recv_ref, acc_ref, a_send, a_recv, o_send, o_recv,
+):
+    rows, width = x_ref.shape
+    seq = 2 * rows
+    local = wout_ref.shape[0]
+    block = rows // 2
+    piece = rows // 4
+    side = lax.axis_index("tensor")
+    partner = peer_x()
+    own = pl.multiple_of(side * rows, rows)
+    theirs = pl.multiple_of((1 - side) * rows, rows)
+    greet([partner])
+
+    def a1_copy(base, b):
+        part = a1_ref.at[pl.ds(pl.multiple_of(base + b * piece, piece), piece)]
+        return remote(part, part, a_send.at[b], a_recv.at[b], partner)
+
+    gain = gain_ref[...].astype(F32)
+    shift = shift_ref[...].astype(F32)
+    for b in range(4):
+        xhat, _ = norm_parts(x_ref[pl.ds(b * piece, piece)].astype(F32))
+        at = pl.ds(pl.multiple_of(own + b * piece, piece), piece)
+        a1_ref[at] = (xhat * gain + shift).astype(BF16)
+        a1_copy(own, b).start()
+
+    def project(base, count):
+        at = pl.ds(pl.multiple_of(base, block), count)
+        left = a1_ref[at]
+        for part in range(3):
+            cols = pl.ds(part * local, local)
+            qkv_ref[at, cols] = (dot_nn(left, wqkv_ref[:, cols]) + bias_ref[:, cols]).astype(BF16)
+
+    project(own, rows)
+
+    for i in range(4):
+        lo = i * block
+        keys = lo + block
+        is_theirs = side == (1 if i < 2 else 0)
+        at = pl.ds(lo, block)
+
+        @pl.when(is_theirs)
+        def _():
+            for b in (2 * (i % 2), 2 * (i % 2) + 1):
+                a1_copy(theirs, b).wait_recv()
+            project(lo, block)
+
+        same = segc_ref[at] == segr_ref[:, pl.ds(0, keys)]
+        q_pos = lo + lax.broadcasted_iota(jnp.int32, (block, keys), 0)
+        k_pos = lax.broadcasted_iota(jnp.int32, (block, keys), 1)
+        mask_ref[:, pl.ds(0, keys)] = jnp.where(same & (q_pos >= k_pos), 0.0, -1e30)
+
+        def pair(hp, _):
+            base = pl.multiple_of(hp * 2 * HEAD_DIM, 2 * HEAD_DIM)
+            cols = pl.ds(base, 2 * HEAD_DIM)
+            q2 = qkv_ref[at, cols]
+            k2 = qkv_ref[pl.ds(0, keys), pl.ds(pl.multiple_of(local + base, 128), 2 * HEAD_DIM)]
+            v2 = qkv_ref[pl.ds(0, keys), pl.ds(pl.multiple_of(2 * local + base, 128), 2 * HEAD_DIM)]
+            outs = []
+            for h in range(2):
+                scores = dot_nt(only_head(q2, h), k2) * HEAD_DIM**-0.5 + mask_ref[:, pl.ds(0, keys)]
+                weights = jnp.exp(scores - jnp.max(scores, axis=-1, keepdims=True))
+                probs = weights * (1.0 / jnp.sum(weights, axis=-1, keepdims=True))
+                outs.append(dot_nn(probs.astype(BF16), v2))
+            mix_ref[at, cols] = jnp.where(head_lanes(0), outs[0], outs[1]).astype(BF16)
+            return 0
+
+        lax.fori_loop(0, local // (2 * HEAD_DIM), pair, 0)
+        product = dot_nn(mix_ref[at], wout_ref[...])
+
+        @pl.when(is_theirs)
+        def _():
+            send_ref[i % 2] = product.astype(BF16)
+            remote(send_ref.at[i % 2], recv_ref.at[i % 2], o_send.at[i % 2], o_recv.at[i % 2], partner).start()
+
+        @pl.when(jnp.logical_not(is_theirs))
+        def _():
+            acc_ref[pl.ds((i % 2) * block, block)] = product
+
+    for j in range(2):
+        at = pl.ds(j * block, block)
+        remote(send_ref.at[j], recv_ref.at[j], o_send.at[j], o_recv.at[j], partner).wait()
+        h_ref[at] = (
+            x_ref[at].astype(F32) + (acc_ref[at] + recv_ref[j].astype(F32)) + ob_ref[...].astype(F32)
+        )
+    for b in range(4):
+        a1_copy(own, b).wait_send()
+
+
+def attend_call(x, gain, shift, wqkv, bias, segc, segr, wout, ob):
+    rows, width = x.shape
+    local = wout.shape[0]
+    seq = 2 * rows
+    block = rows // 2
+    vm = pl.BlockSpec(memory_space=pltpu.VMEM)
+    return pl.pallas_call(
+        attend_kernel,
+        out_shape=(
+            jax.ShapeDtypeStruct((seq, width), BF16),
+            jax.ShapeDtypeStruct((seq, 3 * local), BF16),
+            jax.ShapeDtypeStruct((seq, local), BF16),
+            jax.ShapeDtypeStruct((rows, width), F32),
+        ),
+        in_specs=[vm] * 9,
+        out_specs=(vm,) * 4,
+        scratch_shapes=[
+            pltpu.VMEM((block, seq), F32),
+            pltpu.VMEM((2, block, width), BF16),
+            pltpu.VMEM((2, block, width), BF16),
+            pltpu.VMEM((rows, width), F32),
+            pltpu.SemaphoreType.DMA((4,)),
+            pltpu.SemaphoreType.DMA((4,)),
+            pltpu.SemaphoreType.DMA((2,)),
+            pltpu.SemaphoreType.DMA((2,)),
+        ],
+        compiler_params=pltpu.CompilerParams(
+            collective_id=0, has_side_effects=True, vmem_limit_bytes=VMEM_LIMIT
+        ),
+        name="attend_forward",
+    )(x, gain, shift, wqkv, bias, segc, segr, wout, ob)
+
+
+GATHER_CHUNKS = 2
+
+
+def gather_kernel(up_ref, down_ref, ub_ref, up_o, down_o, ub_o, x_s, x_r, z_s, z_r, y_s, y_r, c_s, c_r, b_s, b_r):
+    z, y, core, side = place()
+    greet([peer_x(), peer_y(), peer_core()] + [peer_z(k) for k in (1, 2, 3)])
+    pieces = 16
+    up_rows = up_ref.shape[0] // pieces // GATHER_CHUNKS
+    down_rows = down_ref.shape[0] // pieces // GATHER_CHUNKS
+
+    def views(up, down, dp, q):
+        lo_u = pl.multiple_of((dp * GATHER_CHUNKS + q) * up_rows, up_rows)
+        lo_d = pl.multiple_of((dp * GATHER_CHUNKS + q) * down_rows, down_rows)
+        return up.at[pl.ds(lo_u, up_rows)], down.at[pl.ds(lo_d, down_rows)]
+
+    def copies(dp, q, send, recv, peer, source=None):
+        src = views(*(source or (up_o, down_o)), dp, q)
+        dst = views(up_o, down_o, dp, q)
+        return [remote(src[a], dst[a], send.at[a], recv.at[a], peer) for a in range(2)]
+
+    def piece(zz, yy, cc):
+        return zz * 4 + yy * 2 + cc
+
+    def x_copies(q):
+        return copies(piece(z, y, core), q, x_s.at[q], x_r.at[q], peer_x(), (up_ref, down_ref))
+
+    def z_sends(q, k):
+        return copies(piece(z, y, core), q, z_s.at[q, k], z_r.at[q, k], peer_z(k))
+
+    def z_recvs(q, k):
+        return copies(piece((z + 4 - k) % 4, y, core), q, z_s.at[q, k], z_r.at[q, k], peer_z(k))
+
+    def y_copies(q, k, yy):
+        return copies(piece((z + 4 - k) % 4, yy, core), q, y_s.at[q, k], y_r.at[q, k], peer_y())
+
+    def c_copies(q, k, yy, cc):
+        slot = (yy + y) % 2 * 4 + k
+        return copies(piece((z + 4 - k) % 4, yy, cc), q, c_s.at[q, slot], c_r.at[q, slot], peer_core())
+
+    def start(list_of):
+        for copy in list_of:
+            copy.start()
+
+    bias_copy = remote(ub_ref, ub_o, b_s, b_r, peer_x())
+    bias_copy.start()
+    for q in range(GATHER_CHUNKS):
+        start(x_copies(q))
+
+    def first(q):
+        for copy in x_copies(q):
+            copy.wait()
+        for k in (2, 1, 3):
+            start(z_sends(q, k))
+        start(y_copies(q, 0, y))
+        start(c_copies(q, 0, y, core))
+
+    def second(q):
+        for k in (1, 3, 2):
+            for copy in z_recvs(q, k):
+                copy.wait_recv()
+            start(y_copies(q, k, y))
+            start(c_copies(q, k, y, core))
+
+    def third(q):
+        for k in range(4):
+            for copy in y_copies(q, k, 1 - y):
+                copy.wait_recv()
+            start(c_copies(q, k, 1 - y, core))
+
+    def last(q):
+        for k in range(4):
+            for yy in (y, 1 - y):
+                for copy in c_copies(q, k, yy, 1 - core):
+                    copy.wait_recv()
+
+    for n in range(GATHER_CHUNKS + 3):
+        for stage, at in ((first, n), (second, n - 1), (third, n - 2), (last, n - 3)):
+            if 0 <= at < GATHER_CHUNKS:
+                stage(at)
+    for q in range(GATHER_CHUNKS):
+        for k in range(4):
+            if k > 0:
+                for copy in z_sends(q, k):
+                    copy.wait_send()
+            for copy in y_copies(q, k, y):
+                copy.wait_send()
+            for yy in (y, 1 - y):
+                for copy in c_copies(q, k, yy, core):
+                    copy.wait_send()
+    bias_copy.wait()
+
+
+def gather_call(up, down, ub):
+    hbm = pl.BlockSpec(memory_space=pltpu.HBM)
+    q = GATHER_CHUNKS
+    sem = pltpu.SemaphoreType.DMA
+    return pl.pallas_call(
+        gather_kernel,
+        out_shape=tuple(jax.ShapeDtypeStruct(a.shape, a.dtype) for a in (up, down, ub)),
+        in_specs=[hbm] * 3,
+        out_specs=(hbm,) * 3,
+        scratch_shapes=[
+            sem((q, 2)), sem((q, 2)), sem((q, 4, 2)), sem((q, 4, 2)), sem((q, 4, 2)), sem((q, 4, 2)),
+            sem((q, 8, 2)), sem((q, 8, 2)), sem, sem,
+        ],
+        compiler_params=pltpu.CompilerParams(
+            collective_id=1, has_side_effects=True, vmem_limit_bytes=VMEM_LIMIT
+        ),
+        name="gather_weights",
+    )(up, down, ub)
+
+
+HIDDEN_BLOCK = 512
+
+
+def feed_kernel(
+    h_ref, g_ref, gain_ref, shift_ref, db_ref, ub_ref, up_own, down_own, up_oth, down_oth,
+    out_ref, dh_ref, vec_ref, usum_ref, keep_ref, recv_ref,
+    a2_ref, a2t_ref, gt_ref, acc_ref, da2_ref, wu_ref, wd_ref, grad_ref, w_sem, k_sem, s_sem, r_sem,
+):
+    rows, width = h_ref.shape
+    z, y, core, side = place()
+    half = up_own.shape[1] // HIDDEN_BLOCK
+    blocks = 2 * half
+    hb = HIDDEN_BLOCK
+    other = peer_core()
+    greet([other])
+
+    def fetch(j, up, down, slot):
+        at = pl.ds(pl.multiple_of((j % half) * hb, hb), hb)
+        return (
+            pltpu.make_async_copy(up.at[:, at], wu_ref.at[slot], w_sem.at[slot, 0]),
+            pltpu.make_async_copy(down.at[at], wd_ref.at[slot], w_sem.at[slot, 1]),
+        )
+
+    def fetch_start(j, slot):
+        @pl.when(j < half)
+        def _():
+            for copy in fetch(j, up_own, down_own, slot):
+                copy.start()
+
+        @pl.when(j >= half)
+        def _():
+            for copy in fetch(j, up_oth, down_oth, slot):
+                copy.start()
+
+    fetch_start(0, 0)
+    gain = gain_ref[...].astype(F32)
+    xhat, _ = norm_parts(h_ref[...])
+    a2 = (xhat * gain + shift_ref[...].astype(F32)).astype(BF16)
+    a2_ref[...] = a2
+    a2t_ref[...] = a2.T
+    gt_ref[...] = g_ref[...].T
+    acc_ref[...] = jnp.zeros_like(acc_ref)
+    da2_ref[...] = jnp.zeros_like(da2_ref)
+
+    def grad_copies(j, slot):
+        return (
+            pltpu.make_async_copy(grad_ref.at[slot, :, core], keep_ref.at[j], k_sem.at[slot]),
+            remote(grad_ref.at[slot, :, 1 - core], recv_ref.at[j], s_sem.at[slot], r_sem.at[j], other),
+        )
+
+    def step(j, _):
+        slot = j % 2
+        for copy in fetch(j, up_own, down_own, slot):
+            copy.wait()
+
+        @pl.when(j + 1 < blocks)
+        def _():
+            fetch_start(j + 1, 1 - slot)
+
+        wu, wd = wu_ref[slot], wd_ref[slot]
+        u = dot_nn(a2_ref[...], wu) + ub_ref[pl.ds(j, 1)]
+        cube = 0.044715 * u * u * u
+        tanh = jnp.tanh(0.7978845608028654 * (u + cube))
+        hidden = (0.5 * u * (1.0 + tanh)).astype(BF16)
+        slope = 0.5 * (1.0 + tanh) + 0.5 * u * (1.0 - tanh * tanh) * (
+            0.7978845608028654 * (1.0 + 3.0 * 0.044715 * u * u)
+        )
+        acc_ref[...] += dot_nn(hidden, wd)
+        du = (dot_nt(g_ref[...], wd) * slope).astype(BF16)
+        where_side = jnp.where(j < half, side, 1 - side)
+        usum_ref[pl.ds(where_side * half + j % half, 1)] = jnp.sum(du.astype(F32), axis=0, keepdims=True)
+        da2_ref[...] += dot_nt(du, wu)
+
+        @pl.when(j >= 2)
+        def _():
+            local, far = grad_copies(j - 2, slot)
+            local.wait()
+            far.wait_send()
+
+        grad_ref[slot, :, :, :, pl.ds(0, hb)] = dot_nn(a2t_ref[...], du).astype(BF16).reshape(8, 2, 64, hb)
+        grad_ref[slot, :, :, :, pl.ds(hb, hb)] = dot_nn(gt_ref[...], hidden).astype(BF16).reshape(8, 2, 64, hb)
+        for copy in grad_copies(j, slot):
+            copy.start()
+        return 0
+
+    lax.fori_loop(0, blocks, step, 0)
+
+    piece = rows // 4
+    sums = [jnp.zeros((1, width), F32) for _ in range(4)]
+    for b in range(4):
+        at = pl.ds(b * piece, piece)
+        h = h_ref[at]
+        g = g_ref[at].astype(F32)
+        out_ref[at] = (h + acc_ref[at] + db_ref[...].astype(F32)).astype(BF16)
+        xhat, rstd = norm_parts(h)
+        da2 = da2_ref[at]
+        e = da2 * gain
+        dh = g + rstd * (
+            e - jnp.mean(e, axis=-1, keepdims=True) - xhat * jnp.mean(e * xhat, axis=-1, keepdims=True)
+        )
+        dh_ref[at] = dh
+        for n, term in enumerate((da2 * xhat, da2, dh.astype(BF16).astype(F32), g)):
+            sums[n] = sums[n] + jnp.sum(term, axis=0, keepdims=True)
+    vec_ref[...] = jnp.concatenate(sums + [jnp.zeros((4, width), F32)], axis=0)
+
+    for j in (blocks - 2, blocks - 1):
+        local, far = grad_copies(j, j % 2)
+        local.wait()
+        far.wait_send()
+    for j in range(blocks):
+        grad_copies(j, j % 2)[1].wait_recv()
+
+
+def feed_call(h, g, gain, shift, db, ub, up_own, down_own, up_oth, down_oth):
+    rows, width = h.shape
+    hb = HIDDEN_BLOCK
+    blocks = 2 * up_own.shape[1] // hb
+    vm = pl.BlockSpec(memory_space=pltpu.VMEM)
+    hbm = pl.BlockSpec(memory_space=pltpu.HBM)
+    sem = pltpu.SemaphoreType.DMA
+    grads = jax.ShapeDtypeStruct((blocks, 8, width // 16, 2 * hb), BF16)
+    return pl.pallas_call(
+        feed_kernel,
+        out_shape=(
+            jax.ShapeDtypeStruct((rows, width), BF16),
+            jax.ShapeDtypeStruct((rows, width), F32),
+            jax.ShapeDtypeStruct((8, width), F32),
+            jax.ShapeDtypeStruct((blocks, hb), F32),
+            grads,
+            grads,
+        ),
+        in_specs=[vm] * 6 + [hbm] * 4,
+        out_specs=(vm,) * 4 + (hbm,) * 2,
+        scratch_shapes=[
+            pltpu.VMEM((rows, width), BF16),
+            pltpu.VMEM((width, rows), BF16),
+            pltpu.VMEM((width, rows), BF16),
+            pltpu.VMEM((rows, width), F32),
+            pltpu.VMEM((rows, width), F32),
+            pltpu.VMEM((2, width, hb), BF16),
+            pltpu.VMEM((2, hb, width), BF16),
+            pltpu.VMEM((2, 8, 2, width // 16, 2 * hb), BF16),
+            sem((2, 2)), sem((2,)), sem((2,)), sem((blocks,)),
+        ],
+        compiler_params=pltpu.CompilerParams(
+            collective_id=2, has_side_effects=True, vmem_limit_bytes=VMEM_LIMIT
+        ),
+        name="feed_forward_backward",
+    )(h, g, gain, shift, db, ub, up_own, down_own, up_oth, down_oth)
+
+
+def back_kernel(
+    dh_ref, x_ref, gain_ref, qkv_ref, mix_ref, a1_ref, wout_ref, wqkv_ref, segc_ref, segr_ref,
+    din_ref, vec_ref, keep_ref, recv_ref,
+    dhl_ref, dm_ref, mask_ref, dk_ref, dv_ref, dqkv_ref, acc_ref, send_buf, recv_buf, grad_ref,
+    d_send, d_recv, o_send, o_recv, k_sem, s_sem, r_sem,
+):
+    rows, width = dh_ref.shape
+    seq = 2 * rows
+    local = wout_ref.shape[0]
+    block = rows // 2
+    z, y, core, side = place()
+    partner = peer_x()
+    other = peer_core()
+    own = pl.multiple_of(side * rows, rows)
+    scale = HEAD_DIM**-0.5
+    greet([partner, other])
+
+    def dh_copy(base, b):
+        part = dhl_ref.at[pl.ds(pl.multiple_of(base + b * block, block), block)]
+        return remote(part, part, d_send.at[b], d_recv.at[b], partner)
+
+    dhl_ref[pl.ds(own, rows)] = dh_ref[...].astype(BF16)
+    for b in (1, 0):
+        dh_copy(own, b).start()
+    dk_ref[...] = jnp.zeros_like(dk_ref)
+    dv_ref[...] = jnp.zeros_like(dv_ref)
+
+    for i in (3, 2, 1, 0):
+        lo = i * block
+        keys = lo + block
+        is_theirs = side == (1 if i < 2 else 0)
+        at = pl.ds(lo, block)
+
+        @pl.when(is_theirs)
+        def _():
+            dh_copy((1 - side) * rows, i % 2).wait_recv()
+
+        dm_ref[...] = dot_nt(dhl_ref[at], wout_ref[...]).astype(BF16)
+        same = segc_ref[pl.ds(0, keys)] == segr_ref[:, at]
+        k_pos = lax.broadcasted_iota(jnp.int32, (keys, block), 0)
+        q_pos = lo + lax.broadcasted_iota(jnp.int32, (keys, block), 1)
+        mask_ref[pl.ds(0, keys)] = jnp.where(same & (q_pos >= k_pos), 0.0, -1e30)
+
+        def pair(hp, _):
+            base = pl.multiple_of(hp * 2 * HEAD_DIM, 2 * HEAD_DIM)
+            cols = pl.ds(base, 2 * HEAD_DIM)
+            q2 = qkv_ref[at, cols]
+            k2 = qkv_ref[pl.ds(0, keys), pl.ds(pl.multiple_of(local + base, 128), 2 * HEAD_DIM)]
+            v2 = qkv_ref[pl.ds(0, keys), pl.ds(pl.multiple_of(2 * local + base, 128), 2 * HEAD_DIM)]
+            g2 = dm_ref[:, cols]
+            dq = jnp.zeros((block, 2 * HEAD_DIM), F32)
+            dk = jnp.zeros((keys, 2 * HEAD_DIM), F32)
+            dv = jnp.zeros((keys, 2 * HEAD_DIM), F32)
+            for h in range(2):
+                qh = only_head(q2, h)
+                gh = only_head(g2, h)
+                scores = dot_nt(k2, qh) * scale + mask_ref[pl.ds(0, keys)]
+                weights = jnp.exp(scores - jnp.max(scores, axis=0, keepdims=True))
+                probs = weights * (1.0 / jnp.sum(weights, axis=0, keepdims=True))
+                dprob = dot_nt(v2, gh)
+                row_dot = jnp.sum(probs * dprob, axis=0, keepdims=True)
+                dscore = (probs * (dprob - row_dot)).astype(BF16)
+                dv += dot_nn(probs.astype(BF16), gh)
+                dk += dot_nn(dscore, qh)
+                dq += dot_tn(dscore, only_head(k2, h))
+            dqkv_ref[at, cols] = (dq * scale).astype(BF16)
+            dk_ref[pl.ds(0, keys), cols] += dk
+            dv_ref[pl.ds(0, keys), cols] += dv
+            return 0
+
+        lax.fori_loop(0, local // (2 * HEAD_DIM), pair, 0)
+        dqkv_ref[at, pl.ds(local, local)] = (dk_ref[at] * scale).astype(BF16)
+        dqkv_ref[at, pl.ds(2 * local, local)] = dv_ref[at].astype(BF16)
+        product = dot_nt(dqkv_ref[at], wqkv_ref[...])
+
+        @pl.when(is_theirs)
+        def _():
+            send_buf[i % 2] = product.astype(BF16)
+            remote(send_buf.at[i % 2], recv_buf.at[i % 2], o_send.at[i % 2], o_recv.at[i % 2], partner).start()
+
+        @pl.when(jnp.logical_not(is_theirs))
+        def _():
+            acc_ref[pl.ds((i % 2) * block, block)] = product
+
+    def grad_copies(j):
+        return (
+            pltpu.make_async_copy(grad_ref.at[j, :, core], keep_ref.at[j], k_sem.at[j]),
+            remote(grad_ref.at[j, :, 1 - core], recv_ref.at[j], s_sem.at[j], r_sem.at[j], other),
+        )
+
+    for part in range(4):
+        if part < 3:
+            grad = dot_tn(a1_ref[...], dqkv_ref[:, pl.ds(part * local, local)])
+        else:
+            grad = dot_tn(dhl_ref[...], mix_ref[...])
+        grad_ref[part // 2, :, :, :, pl.ds((part % 2) * local, local)] = grad.astype(BF16).reshape(8, 2, 64, local)
+        if part % 2 == 1:
+            for copy in grad_copies(part // 2):
+                copy.start()
+
+    gain = gain_ref[...].astype(F32)
+    gain_sum = jnp.zeros((1, width), F32)
+    shift_sum = jnp.zeros((1, width), F32)
+    for j in (1, 0):
+        at = pl.ds(j * block, block)
+        remote(send_buf.at[j], recv_buf.at[j], o_send.at[j], o_recv.at[j], partner).wait()
+        da1 = acc_ref[at] + recv_buf[j].astype(F32)
+        xhat, rstd = norm_parts(x_ref[at].astype(F32))
+        e = da1 * gain
+        din_ref[at] = dh_ref[at] + rstd * (
+            e - jnp.mean(e, axis=-1, keepdims=True) - xhat * jnp.mean(e * xhat, axis=-1, keepdims=True)
+        )
+        gain_sum = gain_sum + jnp.sum(da1 * xhat, axis=0, keepdims=True)
+        shift_sum = shift_sum + jnp.sum(da1, axis=0, keepdims=True)
+    vec_ref[...] = jnp.zeros_like(vec_ref)
+    vec_ref[pl.ds(0, 1)] = gain_sum
+    vec_ref[pl.ds(1, 1)] = shift_sum
+    q_sum = jnp.sum(dqkv_ref[:, pl.ds(0, local)].astype(F32), axis=0, keepdims=True)
+    v_sum = jnp.sum(dqkv_ref[:, pl.ds(2 * local, local)].astype(F32), axis=0, keepdims=True)
+    cols = pl.ds(pl.multiple_of(side * local, local), local)
+    vec_ref[pl.ds(2, 1), cols] = q_sum
+    vec_ref[pl.ds(3, 1), cols] = v_sum
+
+    for b in range(2):
+        dh_copy(own, b).wait_send()
+    for j in range(2):
+        near, far = grad_copies(j)
+        near.wait()
+        far.wait()
+
+
+def back_call(dh, x, gain, qkv, mix, a1, wout, wqkv, segc, segr):
+    rows, width = dh.shape
+    seq = 2 * rows
+    local = wout.shape[0]
+    block = rows // 2
+    vm = pl.BlockSpec(memory_space=pltpu.VMEM)
+    hbm = pl.BlockSpec(memory_space=pltpu.HBM)
+    sem = pltpu.SemaphoreType.DMA
+    grads = jax.ShapeDtypeStruct((2, 8, width // 16, 2 * local), BF16)
+    return pl.pallas_call(
+        back_kernel,
+        out_shape=(
+            jax.ShapeDtypeStruct((rows, width), F32),
+            jax.ShapeDtypeStruct((8, width), F32),
+            grads,
+            grads,
+        ),
+        in_specs=[vm] * 10,
+        out_specs=(vm,) * 2 + (hbm,) * 2,
+        scratch_shapes=[
+            pltpu.VMEM((seq, width), BF16),
+            pltpu.VMEM((block, local), BF16),
+            pltpu.VMEM((seq, block), F32),
+            pltpu.VMEM((seq, local), F32),
+            pltpu.VMEM((seq, local), F32),
+            pltpu.VMEM((seq, 3 * local), BF16),
+            pltpu.VMEM((rows, width), F32),
+            pltpu.VMEM((2, block, width), BF16),
+            pltpu.VMEM((2, block, width), BF16),
+            pltpu.VMEM((2, 8, 2, width // 16, 2 * local), BF16),
+            sem((2,)), sem((2,)), sem((2,)), sem((2,)), sem((2,)), sem((2,)), sem((2,)),
+        ],
+        compiler_params=pltpu.CompilerParams(
+            collective_id=3, has_side_effects=True, vmem_limit_bytes=VMEM_LIMIT
+        ),
+        name="attend_backward",
+    )(dh, x, gain, qkv, mix, a1, wout, wqkv, segc, segr)
+
+
+def scatter_kernel(n_own, n_other, with_vec, *refs):
+    refs = list(refs)
+    keep_ref, recv_ref = refs[:2]
+    refs = refs[2:]
+    if with_vec:
+        vec_in = refs.pop(0)
+        out_ref, vec_out = refs[:2]
+        refs = refs[2:]
+    else:
+        out_ref = refs.pop(0)
+    (keep_v, recv_v, sum_ref, ybuf, part_ref, zbuf, fin_ref, l_sem, y_s, y_r, z_s, z_r) = refs[:12]
+    refs = refs[12:]
+    if n_other:
+        xsend, xbuf, x_s, x_r = refs[:4]
+        refs = refs[4:]
+    if with_vec:
+        vsum, vrecv, v_s, v_r = refs
+    z, y, core, side = place()
+    nb = n_own + n_other
+    need_x = n_other > 0 or with_vec
+    greet(
+        [peer_y()] + [peer_z(k) for k in (1, 2, 3)] + ([peer_x()] if need_x else [])
+        + ([peer_core()] if with_vec else [])
+    )
+
+    def loads(b):
+        slot = b % 2
+        return (
+            pltpu.make_async_copy(keep_ref.at[b], keep_v.at[slot], l_sem.at[slot, 0]),
+            pltpu.make_async_copy(recv_ref.at[b], recv_v.at[slot], l_sem.at[slot, 1]),
+        )
+
+    def y_copy(b):
+        return remote(sum_ref.at[b, :, 1 - y], ybuf.at[b], y_s.at[b], y_r.at[b], peer_y())
+
+    def z_copy(b, k):
+        return remote(
+            part_ref.at[b, (z + k) % 4], zbuf.at[b, k - 1], z_s.at[b, k - 1], z_r.at[b, k - 1], peer_z(k)
+        )
+
+    def x_copy(b):
+        return remote(xsend.at[b], xbuf.at[b], x_s.at[b], x_r.at[b], peer_x())
+
+    def first(b):
+        for copy in loads(b):
+            copy.wait()
+        total = keep_v[b % 2].astype(F32) + recv_v[b % 2].astype(F32)
+        sum_ref[b] = total.astype(BF16).reshape(sum_ref.shape[1:])
+        y_copy(b).start()
+        if b + 2 < nb:
+            for copy in loads(b + 2):
+                copy.start()
+
+    def second(b):
+        y_copy(b).wait_recv()
+        part_ref[b] = (sum_ref[b, :, y].astype(F32) + ybuf[b].astype(F32)).astype(BF16)
+        for k in (2, 1, 3):
+            z_copy(b, k).start()
+
+    def third(b):
+        for k in (1, 2, 3):
+            z_copy(b, k).wait_recv()
+        total = part_ref[b, z].astype(F32)
+        for k in (1, 2, 3):
+            total = total + zbuf[b, k - 1].astype(F32)
+        if b < n_own:
+            fin_ref[b] = total
+        else:
+            xsend[b - n_own] = total.astype(BF16)
+            x_copy(b - n_own).start()
+
+    def last(b):
+        total = fin_ref[b]
+        if n_other:
+            x_copy(b).wait_recv()
+            total = total + xbuf[b].astype(F32)
+        out_ref[b] = total
+
+    for b in range(min(2, nb)):
+        for copy in loads(b):
+            copy.start()
+
+    if with_vec:
+        count = vec_in.shape[0]
+
+        def v_copy(n, peer, slot):
+            return remote(vsum.at[n], vrecv.at[slot], v_s.at[slot], v_r.at[slot], peer)
+
+        def z_vec(k):
+            return remote(vsum.at[2], vrecv.at[2 + z], v_s.at[2 + k], v_r.at[2 + z], peer_z(k))
+
+        def z_vec_from(zz, k):
+            return remote(vsum.at[2], vrecv.at[2 + zz], v_s.at[2 + k], v_r.at[2 + zz], peer_z(k))
+
+        def vec_step(n):
+            if n == 0:
+                vsum[0] = vec_in[...]
+                v_copy(0, peer_core(), 0).start()
+            elif n == 1:
+                v_copy(0, peer_core(), 0).wait()
+                vsum[1] = vsum[0] + vrecv[0]
+                v_copy(1, peer_y(), 1).start()
+            elif n == 2:
+                v_copy(1, peer_y(), 1).wait()
+                vsum[2] = vsum[1] + vrecv[1]
+                for k in (1, 2, 3):
+                    z_vec(k).start()
+            elif n == 3:
+                for k in (1, 2, 3):
+                    z_vec(k).wait_send()
+                    z_vec_from((z + k) % 4, k).wait_recv()
+                vrecv[2 + z] = vsum[2]
+                vsum[3] = (vrecv[2] + vrecv[3]) + (vrecv[4] + vrecv[5])
+                v_copy(3, peer_x(), 6).start()
+            elif n == 4:
+                v_copy(3, peer_x(), 6).wait()
+                vec_out[...] = vsum[3] + vrecv[6]
+    else:
+
+        def vec_step(n):
+            pass
+
+    for n in range(max(nb + 3, 5)):
+        if n < nb:
+            first(n)
+        vec_step(n)
+        if 0 <= n - 1 < nb:
+            second(n - 1)
+        if 0 <= n - 2 < nb:
+            third(n - 2)
+        if n - 3 >= 0 and n_other and n_own <= n - 3 < nb:
+            last(n - 3 - n_own)
+        if not n_other and 0 <= n - 3 < nb:
+            last(n - 3)
+    for b in range(nb):
+        y_copy(b).wait_send()
+        for k in (1, 2, 3):
+            z_copy(b, k).wait_send()
+    for b in range(n_other):
+        x_copy(b).wait_send()
+
+
+def scatter_call(keep, recv, n_own, n_other, vec, cid):
+    nb, chunks, height, cols = keep.shape
+    vm = pl.BlockSpec(memory_space=pltpu.VMEM)
+    hbm = pl.BlockSpec(memory_space=pltpu.HBM)
+    sem = pltpu.SemaphoreType.DMA
+    with_vec = vec is not None
+    out_shape = [jax.ShapeDtypeStruct((n_own, height, cols), F32)]
+    in_specs = [hbm, hbm]
+    args = [keep, recv]
+    scratch = [
+        pltpu.VMEM((2, chunks, height, cols), BF16),
+        pltpu.VMEM((2, chunks, height, cols), BF16),
+        pltpu.VMEM((nb, 4, 2, height, cols), BF16),
+        pltpu.VMEM((nb, 4, height, cols), BF16),
+        pltpu.VMEM((nb, 4, height, cols), BF16),
+        pltpu.VMEM((nb, 3, height, cols), BF16),
+        pltpu.VMEM((n_own, height, cols), F32),
+        sem((2, 2)), sem((nb,)), sem((nb,)), sem((nb, 3)), sem((nb, 3)),
+    ]
+    if n_other:
+        scratch += [
+            pltpu.VMEM((n_other, height, cols), BF16),
+            pltpu.VMEM((n_other, height, cols), BF16),
+            sem((n_other,)), sem((n_other,)),
+        ]
+    if with_vec:
+        out_shape.append(jax.ShapeDtypeStruct(vec.shape, F32))
+        in_specs.append(vm)
+        args.append(vec)
+        scratch += [pltpu.VMEM((4,) + vec.shape, F32), pltpu.VMEM((7,) + vec.shape, F32), sem((7,)), sem((7,))]
+    return pl.pallas_call(
+        functools.partial(scatter_kernel, n_own, n_other, with_vec),
+        out_shape=tuple(out_shape),
+        in_specs=in_specs,
+        out_specs=(vm,) * len(out_shape),
+        scratch_shapes=scratch,
+        compiler_params=pltpu.CompilerParams(
+            collective_id=cid, has_side_effects=True, vmem_limit_bytes=VMEM_LIMIT
+        ),
+        name="scatter_grads",
+    )(*args)
+
+
+def on_device_pair(
+    inputs, segment_ids, first_gain, first_shift, qkv_weight, qv_bias, out_weight, out_bias,
+    second_gain, second_shift, up_weight, up_bias, down_weight, down_bias, cotangent,
+):
+    rows, _, width = inputs.shape
+    seq = segment_ids.shape[0]
+    local = out_weight.shape[0]
+    hidden = up_weight.shape[1]
+    side = lax.axis_index("tensor")
+    x = inputs.reshape(rows, width)
+    g = cotangent.reshape(rows, width)
+    segc = segment_ids.reshape(seq, 1)
+    segr = segment_ids.reshape(1, seq)
+    row = lambda v: v.reshape(1, width)
+    wqkv = qkv_weight.reshape(width, 3 * local)
+    zero = jnp.zeros((local,), F32)
+    bias = jnp.concatenate([qv_bias[0].astype(F32), zero, qv_bias[1].astype(F32)]).reshape(1, 3 * local)
+
+    up_oth, down_oth, ub_oth = gather_call(up_weight, down_weight, up_bias.reshape(16, hidden // 16))
+    ub = jnp.concatenate([up_bias, ub_oth.reshape(hidden)]).astype(F32).reshape(-1, HIDDEN_BLOCK)
+    a1, qkv, mix, h = attend_call(
+        x, row(first_gain), row(first_shift), wqkv, bias, segc, segr, out_weight, row(out_bias)
+    )
+    layer_output, dh, vec_b, up_sums, keep_m, recv_m = feed_call(
+        h, g, row(second_gain), row(second_shift), row(down_bias), ub, up_weight, down_weight, up_oth, down_oth
+    )
+    half = hidden // HIDDEN_BLOCK
+    (mlp,) = scatter_call(keep_m, recv_m, half, half, None, 4)
+    input_grad, vec_c, keep_a, recv_a = back_call(
+        dh, x, row(first_gain), qkv, mix, a1, out_weight, wqkv, segc, segr
+    )
+    vec = jnp.concatenate([vec_b, vec_c, up_sums.reshape(-1, width), jnp.zeros((4, width), F32)], axis=0)
+    attn, total = scatter_call(keep_a, recv_a, 2, 0, vec, 5)
+
+    height = width // 16
+    up_share = jnp.transpose(mlp[:, :, :HIDDEN_BLOCK], (1, 0, 2)).reshape(height, hidden)
+    down_share = jnp.transpose(mlp[:, :, HIDDEN_BLOCK:], (0, 2, 1)).reshape(hidden, height)
+    qkv_share = jnp.concatenate([attn[0], attn[1][:, :local]], axis=1).reshape(height, 3, local)
+    out_share = attn[1][:, local:].T
+    qv_share = lax.dynamic_slice_in_dim(total[10:12], side * local, local, 1)
+    up_bias_share = lax.dynamic_slice_in_dim(total[16:20].reshape(2 * hidden), side * hidden, hidden, 0)
+    return (
+        layer_output.reshape(rows, 1, width),
+        input_grad.reshape(rows, 1, width),
+        total[8],
+        total[9],
+        qkv_share,
+        qv_share,
+        out_share,
+        total[2],
+        total[0],
+        total[1],
+        up_share,
+        up_bias_share,
+        down_share,
+        total[3],
+    )
+
+
 def solution(mesh):
     in_specs = (
         P("tensor", "dp", None),
@@ -327,6 +1210,7 @@
         P("tensor", "dp"),
         P(),
     )
+    pair = mesh.shape["tensor"] == 2 and mesh.shape["dp"] == Z_SIZE * Y_SIZE * CORES
     return jax.shard_map(
-        on_device, mesh=mesh, in_specs=in_specs, out_specs=out_specs, check_vma=False
-    )
+        on_device_pair if pair else on_device, mesh=mesh, in_specs=in_specs, out_specs=out_specs, check_vma=False
+    )

time: 939 us -> 438 us (0.47)
  waiting for transfers between devices: 586 us -> 0 us
  Pallas kernels: 0 us -> 408 us
  matrix products: 176 us -> 0 us
  other arithmetic: 60.7 us -> 2.89 us
  blocking collectives: 40.2 us -> 0 us
  local copies, waits for them, and re-layouts: 43.1 us -> 24.1 us
  between operations: 15.1 us -> 1.05 us
    reduce_scatter x8 -> x0, waiting for transfers between devices: 465 us -> none  [the longest x1 109 us: on_device(): lax.psum_scatter(up_grad, 'dp', scatter_dimension=0, tiled=True)]
    pallas_call x0 -> x6, Pallas kernels: none -> 408 us  [the longest x2 174 us: scatter_call(): pl.pallas_call(functools.partial(scatter_kernel, n_own, n_other, with_vec...]
    dot_general x26 -> x0, matrix products: 176 us -> none  [the longest x4 32.4 us: rows_contract(): lax.dot_general(left, right, (((0,), (0,)), ((), ())), preferred_element_...]
    all_gather x4 -> x0, waiting for transfers between devices: 121 us -> none  [the longest x1 33.2 us: on_device(): residual_rows = lax.all_gather(residual_low, 'tensor', axis=0, tiled=True)]
    psum x1 -> x0, blocking collectives: 40.2 us -> none  [on_device(): lax.psum((stacked, qv_full, up_full), ('dp', 'tensor'))]
    reduce_sum x13 -> x0, other arithmetic: 29.4 us -> none  [the longest x2 8.49 us: one_block(): row_total = jnp.sum(weights, axis=-1, keepdims=True)]
    convert_element_type x12 -> x2, other arithmetic: 24.3 us -> 1.38 us  [the longest x1 0.76 us: on_device_pair(): qv_bias[0].astype(F32)]
    reshape x0 -> x12, local copies, waits for them, and re-layouts: none -> 9.66 us  [the longest x6 3.58 us: on_device_pair(): row = lambda v: v.reshape(1, width)]
  transfers between devices with their start and end apart: 12 -> 0, of which waited for: 12 -> 0; matrix products, arithmetic and copies ran while one was open for 8% -> 0% of each run, Pallas kernels for 0% -> 0%
where the time goes in v1:
time: 438 us; the launch traced here: 436 us
  Pallas kernels  408 us (93%)
  local copies, waits for them, and re-layouts  24.1 us (6%)
    pallas_call x2, Pallas kernels, scatter_call(): pl.pallas_call(functools.partial(scatter_kernel, n_own, n_other, with_vec...  174 us
    pallas_call x1, Pallas kernels, back_call(): pl.pallas_call(back_kernel, out_shape=(jax.ShapeDtypeStruct((rows, width)...  75 us
    pallas_call x1, Pallas kernels, gather_call(): pl.pallas_call(gather_kernel, out_shape=tuple((jax.ShapeDtypeStruct(a.sha...  65.3 us
    pallas_call x1, Pallas kernels, attend_call(): pl.pallas_call(attend_kernel, out_shape=(jax.ShapeDtypeStruct((seq, width...  55.1 us
    pallas_call x1, Pallas kernels, feed_call(): pl.pallas_call(feed_kernel, out_shape=(jax.ShapeDtypeStruct((rows, width)...  38.6 us
    unnamed x33, local copies, waits for them, and re-layouts  10.1 us

profile of v1, /device:TPU:0, one launch (start us, length us, event | category | flops | bytes accessed | tf_op | source)
XLA Modules:
  0.0 436.2 jit_solution(9459174760239764174)
XLA Ops:
  0.6 0.8 slice_convert_fusion.1
  1.4 0.6 reshape.99.bias_ref
  2.0 3.2 copy.34
  5.3 3.0 copy.35.wqkv_ref
  8.3 1.0 copy.36.segc_ref
  11.1 55.1 %attend_forward.1 = (bf16[1024,1024]{1,0:T(8,128)(2,1)}, bf16[1024,1536]{1,0:T(8,128)(2,1)}, bf16[1024,512]{1,0:T(8,128)(2,1)}, f32[512,1024]{1,0:T(8,128)}) custom-call(bf16[512,1024]{1,0:T(8,128)(2,1)} %bitcast.39, bf16[1,1024]{1,0:T(2,128)(2,1)} %reshape.96.gain_ref, bf16[1,1024]{1,0:T(2,128)(2,1)} %reshape.97.shift_ref, ...), custom_call_target="tpu_custom_call" | custom-call | tf_op jit(solution)/shard_map/attend_forward/pallas_call | solution.py:475
  66.3 65.3 %gather_weights.1 = (bf16[1024,2048]{1,0:T(8,128)(2,1)}, bf16[2048,1024]{1,0:T(8,128)(2,1)}, bf16[16,128]{1,0:T(8,128)(2,1)}) custom-call(bf16[1024,2048]{1,0:T(8,128)(2,1)} %up_own.1, bf16[2048,1024]{1,0:T(8,128)(2,1)} %down_own.1, bf16[16,128]{1,0:T(8,128)(2,1)} %bitcast.51), custom_call_target="tpu_custom_call" | custom-call | tf_op jit(solution)/shard_map/gather_weights/pallas_call | solution.py:598
  131.5 0.7 concatenate.19
  132.2 0.6 maximum_convert_fusion.ub_ref
  134.6 38.6 %feed_forward_backward.1 = (bf16[512,1024]{1,0:T(8,128)(2,1)}, f32[512,1024]{1,0:T(8,128)}, f32[8,1024]{1,0:T(8,128)}, f32[8,512]{1,0:T(8,128)}, bf16[8,8,64,102...) custom-call(f32[512,1024]{1,0:T(8,128)} %get-tuple-element.33.h_ref, bf16[512,1024]{1,0:T(8,128)(2,1)} %bitcast.43, ...), custom_call_target="tpu_custom_call" | custom-call | tf_op jit(solution)/shard_map/feed_forward_backward/pallas_call | solution.py:735
  173.3 75.0 %attend_backward.1 = (f32[512,1024]{1,0:T(8,128)}, f32[8,1024]{1,0:T(8,128)}, bf16[2,8,64,1024]{3,2,1,0:T(8,128)(2,1)}, bf16[2,8,64,1024]{3,2,1,0:T(8,128)(2,1)}) custom-call(f32[512,1024]{1,0:T(8,128)} %get-tuple-element.38.dh_ref, bf16[512,1024]{1,0:T(8,128)(2,1)} %bitcast.40, bf16[1,1024]{1,0:T(2,128)(2,1)} %reshape.96.gain_ref, ...), custom_call_target="tpu_custom_call" | custom-call | tf_op jit(solution)/shard_map/attend_backward/pallas_call | solution.py:905
  248.4 1.5 maximum_maximum_fusion.refs_2_
  249.9 62.6 %scatter_grads.2 = (f32[2,64,1024]{2,1,0:T(8,128)}, f32[24,1024]{1,0:T(8,128)}) custom-call(bf16[2,8,64,1024]{3,2,1,0:T(8,128)(2,1)} %get-tuple-element.43.refs_0_, bf16[2,8,64,1024]{3,2,1,0:T(8,128)(2,1)} %get-tuple-element.44.refs_1_, f32[24,1024]{1,0:T(8,128)} %maximum_maximum_fusion.refs_2_), custom_call_target="tpu_custom_call" | custom-call | tf_op jit(solution)/shard_map/scatter_grads/pallas_call | solution.py:1107
  312.5 1.1 slice_bitcast_fusion.3
  313.6 0.7 slice_bitcast_fusion.4
  314.3 0.8 copy.49
  315.1 0.6 dynamic_slice.7
  315.7 0.6 fusion
  317.0 3.5 copy.41
  320.4 111.5 %scatter_grads.3 = f32[4,64,1024]{2,1,0:T(8,128)} custom-call(bf16[8,8,64,1024]{3,2,1,0:T(8,128)(2,1)} %get-tuple-element.50.refs_0_, bf16[8,8,64,1024]{3,2,1,0:T(8,128)(2,1)} %get-tuple-element.51.refs_1_), custom_call_target="tpu_custom_call" | custom-call | tf_op jit(solution)/shard_map/scatter_grads/pallas_call | solution.py:1107
  432.0 1.4 slice_bitcast_fusion
  433.4 0.8 copy.44
  434.2 0.8 copy.45
  435.0 1.0 copy.52
  (43 shorter events, 4.4 us)
Async XLA Ops:
  5.2 3.1 copy-start.2
  5.2 4.1 copy-start.7
  5.2 4.7 %copy-start.8 = (bf16[1024]{0:T(1024)(128)(2,1)S(1)}, bf16[1024]{0:T(1024)(128)(2,1)}, u32[]{:S(2)}) copy-start(bf16[1024]{0:T(1024)(128)(2,1)} %param.22) | copy-start | bytes 6148
  5.2 5.3 %copy-start.9 = (bf16[1024]{0:T(1024)(128)(2,1)S(1)}, bf16[1024]{0:T(1024)(128)(2,1)}, u32[]{:S(2)}) copy-start(bf16[1024]{0:T(1024)(128)(2,1)} %param.18) | copy-start | bytes 6148
  66.2 66.0 %copy-start.5 = (bf16[2048]{0:T(1024)(128)(2,1)S(1)}, bf16[2048]{0:T(1024)(128)(2,1)}, u32[]{:S(2)}) copy-start(bf16[2048]{0:T(1024)(128)(2,1)} %param.26) | copy-start | bytes 12292
  66.2 66.6 %copy-start.10 = (bf16[1024]{0:T(1024)(128)(2,1)S(1)}, bf16[1024]{0:T(1024)(128)(2,1)}, u32[]{:S(2)}) copy-start(bf16[1024]{0:T(1024)(128)(2,1)} %param.23) | copy-start | bytes 6148
  66.2 67.2 %copy-start.11 = (bf16[1024]{0:T(1024)(128)(2,1)S(1)}, bf16[1024]{0:T(1024)(128)(2,1)}, u32[]{:S(2)}) copy-start(bf16[1024]{0:T(1024)(128)(2,1)} %param.24) | copy-start | bytes 6148
  66.3 67.8 %copy-start.12 = (bf16[1024]{0:T(1024)(128)(2,1)S(1)}, bf16[1024]{0:T(1024)(128)(2,1)}, u32[]{:S(2)}) copy-start(bf16[1024]{0:T(1024)(128)(2,1)} %param.28) | copy-start | bytes 6148
  173.2 75.1 %copy-start.6 = (f32[8,512]{1,0:T(8,128)S(1)}, f32[8,512]{1,0:T(8,128)}, u32[]{:S(2)}) copy-start(f32[8,512]{1,0:T(8,128)} %get-tuple-element.47) | copy-start | bytes 49156
  173.3 75.2 %copy-start.3 = (f32[8,1024]{1,0:T(8,128)S(1)}, f32[8,1024]{1,0:T(8,128)}, u32[]{:S(2)}) copy-start(f32[8,1024]{1,0:T(8,128)} %get-tuple-element.45) | copy-start | bytes 98308
  249.9 67.1 %copy-start = (f32[512,1024]{1,0:T(8,128)S(1)}, f32[512,1024]{1,0:T(8,128)}, u32[]{:S(2)}) copy-start(f32[512,1024]{1,0:T(8,128)} %get-tuple-element.42) | copy-start | bytes 6291460
  312.5 2.6 copy-start.4
  432.0 3.0 copy-start.1
